TPU v7x, 128 devices: a whole 4x4x4 slice. The times are simulated.
128 devices in a mesh: dp: 16 (over z, y_hi, core), expert: 8 (over y_lo, x).
Axes of the slice: x: 4, y: 4 (y_hi: 2, y_lo: 2; y = y_hi * 2 + y_lo), z: 4, core: 2. Of those that a mesh axis runs over, the one named last changes fastest.
Arguments:
- tokens: bfloat16 [1536, 6144], P(('dp', 'expert')), may hold values from -6 to 6
- cotangent: bfloat16 [1536, 6144], P(('dp', 'expert')), may hold values from -6 to 6
- expert_ids: int32 [1536, 2], P('dp'), may hold values from 0 to 7, all different within a row; in each aligned block of 96 rows (0 to 95, 96 to 191, ...) at most 32 rows name the same one
- gate_values: float32 [1536, 2], P('dp'), may hold values from 0.2 to 1
- w_in: bfloat16 [8, 6144, 8192], P('expert', None, 'dp'), may hold values from -0.078125 to 0.078125
- w_out: bfloat16 [8, 8192, 6144], P('expert', 'dp'), may hold values from -0.0625 to 0.0625
Outputs:
- layer_out: bfloat16 [1536, 6144], P(('dp', 'expert'))
- grad_tokens: bfloat16 [1536, 6144], P(('dp', 'expert'))
- grad_in: bfloat16 [8, 6144, 8192], P('expert', None, 'dp')
- grad_out: bfloat16 [8, 8192, 6144], P('expert', 'dp')
Inputs may be any that keep to these rules, and one draw needn't show every extreme that they name: `expert_ids`: A token names 2 different experts. Within the 96 tokens of one dp index no expert is named by more than 32 tokens, and in every draw some expert is named by exactly 32 tokens of some dp index.
All inputs are finite; a program needn't handle non-finite values.
Results may differ from a plain program's by a relative error of at most 0.0058.
Values may be sent and summed in bfloat16 or wider, within the bound.
A program may use at most 192 MiB of HBM per device.

v0:
```python
import jax
import jax.numpy as jnp
from jax import lax
from jax.sharding import PartitionSpec as P


def slot_tables(ids, gates, expert, slot_count):
    chosen = ids == expert
    gate_sum = jnp.sum(jnp.where(chosen, gates, jnp.float32(0.0)), axis=1)
    picked = jnp.any(chosen, axis=1).astype(jnp.int32)
    placed = jnp.cumsum(picked) - 1
    slots = lax.broadcasted_iota(jnp.int32, (slot_count, ids.shape[0]), 0)
    table = ((placed[None, :] == slots) & (picked[None, :] == 1)).astype(jnp.float32)
    return (table, gate_sum)


def unpack(table, slot_rows):
    return jnp.dot(
        table.T, slot_rows, precision=lax.Precision.HIGHEST, preferred_element_type=jnp.float32
    )


def local(tokens, cotangent, expert_ids, gate_values, w_in, w_out):
    group_tokens = expert_ids.shape[0]
    slot_count = max(
        group_tokens // 3, expert_ids.shape[1] * group_tokens // lax.axis_size("expert")
    )
    expert = lax.axis_index("expert")
    table, gate_sum = slot_tables(expert_ids, gate_values, expert, slot_count)
    table_half = table.astype(jnp.bfloat16)
    weight_in = w_in[0]
    weight_out = w_out[0]
    group_in, group_cot = (
        lax.all_gather(tokens, "expert", axis=0, tiled=True),
        lax.all_gather(cotangent, "expert", axis=0, tiled=True),
    )
    packed = jnp.dot(table_half, group_in, preferred_element_type=jnp.float32).astype(jnp.bfloat16)
    rows = lax.all_gather(packed, "dp", axis=0, tiled=True)
    pre = jnp.dot(rows, weight_in, preferred_element_type=jnp.float32)
    hidden = jax.nn.silu(pre).astype(jnp.bfloat16)
    weighted = (gate_sum[:, None] * group_cot).astype(jnp.bfloat16)
    packed_grad = jnp.dot(table_half, weighted, preferred_element_type=jnp.float32).astype(
        jnp.bfloat16
    )
    piece = hidden
    slot_out = lax.psum_scatter(
        jnp.dot(piece, weight_out, preferred_element_type=jnp.float32),
        "dp",
        scatter_dimension=0,
        tiled=True,
    )
    out_term = gate_sum[:, None] * unpack(table, slot_out)
    layer_out = lax.psum_scatter(out_term, "expert", scatter_dimension=0, tiled=True).astype(
        jnp.bfloat16
    )
    row_keep, slot_grad = (
        lax.all_gather(packed, "dp", axis=0, tiled=True),
        lax.all_gather(packed_grad, "dp", axis=0, tiled=True),
    )
    grad_out = jnp.einsum("rf,rd->fd", hidden, slot_grad, preferred_element_type=jnp.float32)
    grad_hidden = jnp.einsum("rd,fd->rf", slot_grad, weight_out, preferred_element_type=jnp.float32)
    sig = jax.nn.sigmoid(pre)
    grad_pre = (grad_hidden * sig * (1.0 + pre * (1.0 - sig))).astype(jnp.bfloat16)
    grad_in = jnp.einsum("rd,rf->df", row_keep, grad_pre, preferred_element_type=jnp.float32)
    piece = grad_pre
    slot_back = lax.psum_scatter(
        jnp.einsum("rf,df->rd", piece, weight_in, preferred_element_type=jnp.float32),
        "dp",
        scatter_dimension=0,
        tiled=True,
    )
    back_term = unpack(table, slot_back)
    grad_tokens = lax.psum_scatter(back_term, "expert", scatter_dimension=0, tiled=True).astype(
        jnp.bfloat16
    )
    return (
        layer_out,
        grad_tokens,
        grad_in.astype(jnp.bfloat16)[None],
        grad_out.astype(jnp.bfloat16)[None],
    )


def solution(mesh):
    placed = (
        P(("dp", "expert"), None),
        P(("dp", "expert"), None),
        P("dp", None),
        P("dp", None),
        P("expert", None, "dp"),
        P("expert", "dp", None),
    )
    return jax.shard_map(
        local,
        mesh=mesh,
        in_specs=placed,
        out_specs=(
            P(("dp", "expert"), None),
            P(("dp", "expert"), None),
            P("expert", None, "dp"),
            P("expert", "dp", None),
        ),
        check_vma=False,
    )
```

profile of v0, /device:TPU:0, one launch (start us, length us, event | category | flops | bytes accessed | tf_op | source)
XLA Modules:
  0.0 589.7 jit_solution(5294595046763693529)
XLA Ops:
  8.7 0.7 fusion.34
  9.8 42.8 %all-gather.11.cloned.1.call-done = bf16[8,12,6144]{2,1,0:T(8,128)(2,1)} async-done(((bf16[1,12,6144]{2,1,0:T(8,128)(2,1)}), bf16[8,12,6144]{2,1,0:T(8,128)(2,1)}) %all-gather.11.cloned.1.call-update) | async-done | bytes 1179664 | tf_op jit(solution)/shard_map/all_gather | solution.py:34
  52.6 1.5 reshape.48
  54.1 1.0 convolution_convert_fusion.3
  55.3 0.7 select_reduce_fusion
  56.0 38.0 %all-gather.13.cloned.1.call-done = bf16[8,12,6144]{2,1,0:T(8,128)(2,1)} async-done(((bf16[1,12,6144]{2,1,0:T(8,128)(2,1)}), bf16[8,12,6144]{2,1,0:T(8,128)(2,1)}) %all-gather.13.cloned.1.call-update) | async-done | bytes 1179664 | tf_op jit(solution)/shard_map/all_gather | solution.py:35
  94.0 1.5 reshape.51
  95.5 1.1 convolution_convert_fusion.2
  96.7 63.9 %all-gather.7.cloned.1.call-done = bf16[512,6144]{1,0:T(8,128)(2,1)} async-done(((bf16[32,6144]{1,0:T(8,128)(2,1)}), bf16[512,6144]{1,0:T(8,128)(2,1)}) %all-gather.7.cloned.1.call-update) | async-done | bytes 6291472 | tf_op jit(solution)/shard_map/all_gather | solution.py:38
  160.6 7.5 %fusion.10 = f32[512,512]{1,0:T(8,128)S(1)} fusion(bf16[512,6144]{1,0:T(8,128)(2,1)} %all-gather.7.cloned.1.call-done, bf16[1,6144,512]{2,1,0:T(8,128)(2,1)} %param.10), kind=kOutput, calls=%fused_computation.13 | convolution fusion | flops 3221225472 | bytes 13631488 | tf_op jit(solution)/shard_map/dot_general | solution.py:39
  168.1 9.3 %fusion.6 = f32[512,6144]{1,0:T(8,128)} fusion(bf16[1,512,6144]{2,1,0:T(8,128)(2,1)} %param.11, f32[512,512]{1,0:T(8,128)S(1)} %fusion.10), kind=kOutput, calls=%fused_computation.9 | convolution fusion | flops 3222536192 | bytes 19922944 | tf_op jit(solution)/shard_map/dot_general | solution.py:47
  177.6 47.9 %all-gather.9.cloned.1.call-done = bf16[512,6144]{1,0:T(8,128)(2,1)} async-done(((bf16[32,6144]{1,0:T(8,128)(2,1)}), bf16[512,6144]{1,0:T(8,128)(2,1)}) %all-gather.9.cloned.1.call-update) | async-done | bytes 6291472 | tf_op jit(solution)/shard_map/all_gather | solution.py:58
  225.5 8.2 %fusion.18 = bf16[512,512]{1,0:T(8,128)(2,1)S(1)} fusion(bf16[512,6144]{1,0:T(8,128)(2,1)} %all-gather.9.cloned.1.call-done, bf16[1,512,6144]{2,1,0:T(8,128)(2,1)} %param.11, f32[512,512]{1,0:T(8,128)S(1)} %fusion.10), kind=kOutput, calls=%fused_computation.18 | convolution fusion | flops 3223584768 | bytes 14155776 | tf_op jit(solution)/shard_map/rd,fd->rf/dot_general | solution.py:61
  233.7 11.0 %fusion.8 = f32[512,6144]{1,0:T(8,128)} fusion(bf16[512,512]{1,0:T(8,128)(2,1)S(1)} %fusion.18, bf16[1,6144,512]{2,1,0:T(8,128)(2,1)} %param.10), kind=kOutput, calls=%fused_computation.11 | convolution fusion | flops 3221225472 | bytes 19398656 | tf_op jit(solution)/shard_map/rf,df->rd/dot_general | solution.py:67
  246.6 9.0 %fusion.2 = bf16[1,6144,512]{2,1,0:T(8,128)(2,1)} fusion(bf16[512,6144]{1,0:T(8,128)(2,1)} %all-gather.7.cloned.1.call-done, bf16[512,512]{1,0:T(8,128)(2,1)S(1)} %fusion.18), kind=kOutput, calls=%fused_computation.2 | convolution fusion | flops 3224371200 | bytes 13107200 | tf_op jit(solution)/shard_map/rd,rf->df/dot_general | solution.py:64
  255.7 94.2 %reduce-scatter.7.cloned.1.call-done = f32[32,6144]{1,0:T(8,128)} async-done(((f32[512,6144]{1,0:T(8,128)}), f32[32,6144]{1,0:T(8,128)}) %reduce-scatter.7.cloned.1.call-update) | async-done | bytes 786448 | tf_op jit(solution)/shard_map/reduce_scatter | solution.py:46
  349.9 2.3 convolution_multiply_fusion
  352.1 122.6 %reduce-scatter.9.cloned.1.call-done = f32[32,6144]{1,0:T(8,128)} async-done(((f32[512,6144]{1,0:T(8,128)}), f32[32,6144]{1,0:T(8,128)}) %reduce-scatter.9.cloned.1.call-update) | async-done | bytes 786448 | tf_op jit(solution)/shard_map/reduce_scatter | solution.py:66
  474.7 3.7 fusion.23
  478.4 74.8 %fusion.35 = (f32[16,6144]{1,0:T(8,128)}, f32[16,6144]{1,0:T(8,128)}) fusion(f32[96,6144]{1,0:T(8,128)S(1)} %convolution_multiply_fusion, f32[96,6144]{1,0:T(8,128)} %fusion.23), kind=kCustom, calls=%all-reduce-scatter.2 | all-reduce-scatter fusion | flops 1572865 | bytes 5505536
  553.2 1.0 slice.1
  554.2 1.0 convert.2
  555.3 2.6 collective-permute-start.2
  557.9 2.8 collective-permute-start.3
  560.7 8.2 %fusion.3 = bf16[1,512,6144]{2,1,0:T(8,128)(2,1)} fusion(bf16[512,6144]{1,0:T(8,128)(2,1)} %all-gather.9.cloned.1.call-done, f32[512,512]{1,0:T(8,128)S(1)} %fusion.10), kind=kOutput, calls=%fused_computation.3 | convolution fusion | flops 3225681920 | bytes 13631488 | tf_op jit(solution)/shard_map/rf,rd->fd/dot_general | solution.py:60
  569.0 4.7 collective-permute-start
  573.7 3.3 collective-permute-start.1
  577.1 1.1 concatenate.1
  578.1 0.7 dynamic-slice_convert_fusion
  578.9 2.2 collective-permute-done.1
  581.1 1.1 concatenate
  582.2 0.7 dynamic-slice_convert_fusion.1
  (28 shorter events, 3.5 us)
Async XLA Ops:
  7.2 45.4 %all-gather.11.cloned.1.call-start = ((), (), s32[]{:S(2)}) async-start(), calls=%async_computation.6 | async-start | bytes 1769472 | tf_op jit(solution)/shard_map/all_gather | solution.py:34
  7.9 86.1 %all-gather.13.cloned.1.call-start = ((), (), s32[]{:S(2)}) async-start(), calls=%async_computation.7 | async-start | bytes 1769472 | tf_op jit(solution)/shard_map/all_gather | solution.py:35
  8.6 152.0 %all-gather.7.cloned.1.call-start = ((), (), s32[]{:S(2)}) async-start(), calls=%async_computation.2 | async-start | bytes 6684672 | tf_op jit(solution)/shard_map/all_gather | solution.py:38
  55.2 170.3 %all-gather.9.cloned.1.call-start = ((), (), s32[]{:S(2)}) async-start(), calls=%async_computation.4 | async-start | bytes 6684672 | tf_op jit(solution)/shard_map/all_gather | solution.py:58
  96.7 253.2 %reduce-scatter.7.cloned.1.call-start = ((), (), s32[]{:S(2)}) async-start(), calls=%async_computation.3 | async-start | bytes 13369344 | tf_op jit(solution)/shard_map/reduce_scatter | solution.py:46
  177.4 297.4 %reduce-scatter.9.cloned.1.call-start = ((), (), s32[]{:S(2)}) async-start(), calls=%async_computation.5 | async-start | bytes 13369344 | tf_op jit(solution)/shard_map/reduce_scatter | solution.py:66
  244.7 0.7 copy-start.2
  555.3 13.7 %copy-start = (f32[16,6144]{1,0:T(8,128)S(1)}, f32[16,6144]{1,0:T(8,128)}, u32[]{:S(2)}) copy-start(f32[16,6144]{1,0:T(8,128)} %get-tuple-element.6) | copy-start | bytes 1179652
  555.3 21.8 %copy-start.1 = (f32[16,6144]{1,0:T(8,128)S(1)}, f32[16,6144]{1,0:T(8,128)}, u32[]{:S(2)}) copy-start(f32[16,6144]{1,0:T(8,128)} %get-tuple-element.7) | copy-start | bytes 1179652
  555.3 21.8 %collective-permute-start.2 = (bf16[16,6144]{1,0:T(8,128)(2,1)S(1)}, bf16[16,6144]{1,0:T(8,128)(2,1)S(1)}, u32[]{:S(2)}, u32[]{:S(2)}) collective-permute-start(bf16[16,6144]{1,0:T(8,128)(2,1)S(1)} %convert.2), channel_id=1, source_target_pairs={{0,1},{1,2},{2,3},{3,4},{4,5},{5,6},{6,7},{8,9},{9,10},{10,11},{11... | collective-permute-start | bytes 589832
  557.9 19.1 %collective-permute-start.3 = (bf16[12,6144]{1,0:T(8,128)(2,1)S(1)}, bf16[12,6144]{1,0:T(8,128)(2,1)S(1)}, u32[]{:S(2)}, u32[]{:S(2)}) collective-permute-start(bf16[12,6144]{1,0:T(8,128)(2,1)S(1)} %slice.1), channel_id=1, source_target_pairs={{0,2},{1,3},{2,4},{3,5},{4,6},{5,7},{8,10},{9,11},{10,12},{11,13},... | collective-permute-start | bytes 442376
  569.0 12.1 %collective-permute-start = (bf16[16,6144]{1,0:T(8,128)(2,1)S(1)}, bf16[16,6144]{1,0:T(8,128)(2,1)S(1)}, u32[]{:S(2)}, u32[]{:S(2)}) collective-permute-start(bf16[16,6144]{1,0:T(8,128)(2,1)S(1)} %convert.1), channel_id=1, source_target_pairs={{0,1},{1,2},{2,3},{3,4},{4,5},{5,6},{6,7},{8,9},{9,10},{10,11},{11... | collective-permute-start | bytes 589832
  573.7 7.4 %collective-permute-start.1 = (bf16[12,6144]{1,0:T(8,128)(2,1)S(1)}, bf16[12,6144]{1,0:T(8,128)(2,1)S(1)}, u32[]{:S(2)}, u32[]{:S(2)}) collective-permute-start(bf16[12,6144]{1,0:T(8,128)(2,1)S(1)} %slice), channel_id=1, source_target_pairs={{0,2},{1,3},{2,4},{3,5},{4,6},{5,7},{8,10},{9,11},{10,12},{11,13},... | collective-permute-start | bytes 442376
Sparse Core Ops, SparseCore 0:
  9.6 42.9 all-gather.10
  54.2 39.7 all-gather.12
  97.1 63.5 all-gather.6
  163.5 61.9 all-gather.8
  229.6 120.1 reduce-scatter.6
  354.0 120.6 reduce-scatter.8
where the time goes:
time: 591 us; the launch traced here: 590 us
  waiting for transfers between devices  413 us (70%)
  blocking collectives  74.8 us (13%)
  matrix products  61.3 us (10%)
  between operations  14.9 us (3%)
  starting transfers between devices  13.8 us (2%)
  local copies, waits for them, and re-layouts  9.04 us (2%)
    reduce_scatter x1, waiting for transfers between devices, local(): lax.psum_scatter(jnp.einsum('rf,df->rd', piece, weight_in, preferred_elem...  123 us
    reduce_scatter x1, waiting for transfers between devices, local(): lax.psum_scatter(jnp.dot(piece, weight_out, preferred_element_type=jnp.fl...  94.2 us
    unnamed x1, blocking collectives  74.8 us
    all_gather x1, waiting for transfers between devices, local(): rows = lax.all_gather(packed, 'dp', axis=0, tiled=True)  63.9 us
    all_gather x1, waiting for transfers between devices, local(): lax.all_gather(packed_grad, 'dp', axis=0, tiled=True)  47.9 us
    all_gather x1, waiting for transfers between devices, local(): lax.all_gather(tokens, 'expert', axis=0, tiled=True)  42.8 us
    all_gather x1, waiting for transfers between devices, local(): lax.all_gather(cotangent, 'expert', axis=0, tiled=True)  38 us
    unnamed x4, starting transfers between devices  13.4 us
  transfers between devices with their start and end apart: 10, of which 7 were waited for; matrix products, arithmetic and copies ran while one was open for 11% of the time, Pallas kernels for 0%

commit v1 on v0

v1 whole, which is shorter than its diff:
```python
import functools
import jax
import jax.numpy as jnp
from jax import lax
from jax.experimental import pallas as pl
from jax.experimental.pallas import tpu as pltpu
from jax.sharding import PartitionSpec as P

D = 6144
HID = 512
CAP = 32
TOK = 96
NC = 6
CW = D // NC
QW = CW // 4
ROWS = 512
HALF = 256
DEP = 4
LAG4, LAG5, LAG6 = 1, 2, 3
OFF = NC + LAG6
L2, L3, L4, L5, L6 = 1, 2, 3, 4, 5
STEPS = OFF + 2 * NC + L6
MESH = pl.DeviceIdType.MESH
F32, BF16 = jnp.float32, jnp.bfloat16


def rem(a, b):
    return lax.rem(a, jnp.int32(b))


def at16(v, m=32):
    return pl.multiple_of(v, m)


def dot(a, b, dims=((1,), (0,)), precision=None):
    return lax.dot_general(a, b, (dims, ((), ())), precision=precision, preferred_element_type=F32)


def done(ref, sem):
    pltpu.make_async_copy(ref, ref, sem).wait()


def exchange(
    x_ref, ids_ref, gates_ref, win_hbm, wout_hbm,
    out_ref, rg_hbm, hid, gp,
    win, wout, G, R, pre, gh, A, grep, gslot,
    SB, PO, RB, SS, Z2, Z1, YS, YR, TF, EB, ER,
    w_sem, ge_s, ge_r, ag_s, y_r, zm_r, zp_r, z2m_r, z2p_r, sib_r, hbm_s,
    sb_s, rb_r, ss_s, rz2m_r, rz2p_r, rz1m_r, rz1p_r, ys_s, yr_r, eb_s, er_r,
):
    dp, e = lax.axis_index("dp"), lax.axis_index("expert")
    z, yh, c = dp // 4, (dp // 2) % 2, dp % 2

    def at(zz, yy, cc):
        return (zz * 4 + yy * 2 + cc, e)

    zn, zp_, zo = rem(z + 1, 4), rem(z + 3, 4), rem(z + 2, 4)
    up, down, across, sib = at(zn, yh, c), at(zp_, yh, c), at(z, 1 - yh, c), at(z, yh, 1 - c)
    peers = [rem(e + d, 8) for d in range(1, 8)]

    def send(src, dst, ss, rs, to):
        pltpu.make_async_remote_copy(
            src_ref=src, dst_ref=dst, send_sem=ss, recv_sem=rs, device_id=to, device_id_type=MESH
        ).start()

    load_in = pltpu.make_async_copy(win_hbm, win, w_sem.at[0])
    load_out = pltpu.make_async_copy(wout_hbm, wout, w_sem.at[1])
    load_in.start()
    load_out.start()

    barrier = pltpu.get_barrier_semaphore()
    for to in [up, down, across, sib] + [(dp, p) for p in peers]:
        pl.semaphore_signal(barrier, inc=1, device_id=to, device_id_type=MESH)
    pl.semaphore_wait(barrier, 11)

    mine = pl.ds(at16(e * 48, 16), 48)

    def a1(g):
        for p in peers:
            send(x_ref.at[g], G.at[g, mine], ge_s.at[g], ge_r.at[g], (dp, p))
        G[g, mine] = x_ref[g]

    a1(0)
    a1(1)

    chosen = ids_ref[...] == e
    gsum = jnp.sum(jnp.where(chosen, gates_ref[...], 0.0), axis=1, keepdims=True)
    picked = jnp.max(jnp.where(chosen, 1.0, 0.0), axis=1, keepdims=True)
    row = lax.broadcasted_iota(jnp.int32, (TOK, TOK), 0)
    col = lax.broadcasted_iota(jnp.int32, (TOK, TOK), 1)
    tri = jnp.where(row >= col, 1.0, 0.0).astype(BF16)
    pickb = jnp.broadcast_to(picked, (TOK, 128))
    place = dot(tri, pickb.astype(BF16)) - 1.0
    slots = lax.broadcasted_iota(jnp.int32, (TOK, 128), 1)
    spread = jnp.bitwise_and(slots, 31).astype(F32)
    table = jnp.where(place == spread, pickb, 0.0)
    r4 = lax.broadcasted_iota(jnp.int32, (4 * TOK, TOK), 0)
    t4 = lax.broadcasted_iota(jnp.int32, (4 * TOK, TOK), 1)
    widen = jnp.where(jnp.right_shift(r4, 2) == t4, 1.0, 0.0)
    q_r = jnp.bitwise_and(lax.broadcasted_iota(jnp.int32, (4 * TOK, 128), 0), 3)
    q_c = jnp.right_shift(lax.broadcasted_iota(jnp.int32, (4 * TOK, 128), 1), 5)
    wide = dot(widen.astype(BF16), table.astype(BF16))
    A[...] = jnp.where(q_r == q_c, wide, 0.0).astype(BF16)
    gsb = jnp.broadcast_to(gsum, (TOK, 128))
    grep[...] = dot(widen, gsb, precision=lax.Precision.HIGHEST)
    gslot[...] = dot(table, gsb, ((0,), (0,)), precision=lax.Precision.HIGHEST)

    pre[...] = jnp.zeros_like(pre)
    gh[...] = jnp.zeros_like(gh)

    def block(zz, yy, n=32):
        return pl.ds(at16((c * 8 + zz * 2 + yy) * 32), n)

    def to_sib(g, where):
        send(R.at[g, where], R.at[g, where], ag_s.at[g], sib_r.at[g], sib)

    def a2(g):
        done(G.at[g, pl.ds(0, 336)], ge_r.at[g])
        scale = jnp.where(g < NC, 1.0, grep[...][:, :1])
        v = (G[g].astype(F32) * scale).astype(BF16)
        packed = dot(A[...], v, ((0,), (0,))).astype(BF16)
        own = block(z, yh)
        for q in range(4):
            R[g, own, q * QW : (q + 1) * QW] = packed[q * 32 : (q + 1) * 32]
        me = R.at[g, own]
        send(me, me, ag_s.at[g], y_r.at[g], across)
        send(me, me, ag_s.at[g], zm_r.at[g], up)
        send(me, me, ag_s.at[g], zp_r.at[g], down)
        to_sib(g, own)

    def a3(g):
        theirs = block(z, 1 - yh)
        b = R.at[g, theirs]
        done(b, y_r.at[g])
        send(b, b, ag_s.at[g], zm_r.at[g], up)
        send(b, b, ag_s.at[g], zp_r.at[g], down)
        to_sib(g, theirs)

    def a4(g):
        low = block(zp_, 0, 64)
        done(R.at[g, low], zm_r.at[g])
        b = R.at[g, block(zp_, 0)]
        send(b, b, ag_s.at[g], z2m_r.at[g], up)
        to_sib(g, low)
        high = block(zn, 0, 64)
        done(R.at[g, high], zp_r.at[g])
        b = R.at[g, block(zn, 1)]
        send(b, b, ag_s.at[g], z2p_r.at[g], down)
        to_sib(g, high)

    def a5(g):
        done(R.at[g, block(zo, 0)], z2m_r.at[g])
        done(R.at[g, block(zo, 1)], z2p_r.at[g])
        to_sib(g, block(zo, 0, 64))

    def a6(g):
        done(R.at[g, pl.ds(at16((1 - c) * HALF), HALF)], sib_r.at[g])
        pltpu.make_async_copy(R.at[g], rg_hbm.at[g], hbm_s.at[g]).start()

        @pl.when(g == 0)
        def _():
            load_in.wait()
            load_out.wait()

        @pl.when(g < NC)
        def _():
            pre[...] += dot(R[g], win[pl.ds(at16(g * CW, CW), CW), :])

        @pl.when(g >= NC)
        def _():
            gh[...] += dot(R[g], wout[:, pl.ds(at16((g - NC) * CW, CW), CW)], ((1,), (1,)))

        @pl.when(g == NC - 1)
        def _():
            v = pre[...]
            hid[...] = (v * jax.nn.sigmoid(v)).astype(BF16)

        @pl.when(g == 2 * NC - 1)
        def _():
            v = pre[...]
            s = jax.nn.sigmoid(v)
            gp[...] = (gh[...] * s * (1.0 + v * (1.0 - s))).astype(BF16)

    ours, others = pl.ds(at16(c * HALF), HALF), pl.ds(at16((1 - c) * HALF), HALF)

    def c1(h):
        two, slot = rem(h, 2), rem(h, DEP)

        @pl.when(h >= 2)
        def _():
            done(SB.at[two], sb_s.at[two])

        def product(lhs, w, dims):
            SB[two] = dot(lhs[others, :], w, dims).astype(BF16)
            send(SB.at[two], RB.at[slot], sb_s.at[two], rb_r.at[slot], sib)
            PO[...] = dot(lhs[ours, :], w, dims)

        @pl.when(h < NC)
        def _():
            product(hid, wout[:, pl.ds(at16(h * CW, CW), CW)], ((1,), (0,)))

        @pl.when(h >= NC)
        def _():
            product(gp, win[pl.ds(at16((h - NC) * CW, CW), CW), :], ((1,), (1,)))

    def part(zz, yy, n=32):
        return pl.ds(at16((zz * 2 + yy) * 32), n)

    def c2(h):
        slot = rem(h, DEP)

        @pl.when(h >= DEP)
        def _():
            done(SS.at[slot, pl.ds(0, 192)], ss_s.at[slot])

        done(RB.at[slot], rb_r.at[slot])
        SS[slot] = (PO[...] + RB[slot].astype(F32)).astype(BF16)
        s = ss_s.at[slot]
        send(SS.at[slot, part(zo, 0)], Z2.at[slot, 0], s, rz2m_r.at[slot], up)
        send(SS.at[slot, part(zo, 1)], Z2.at[slot, 1], s, rz2p_r.at[slot], down)
        send(SS.at[slot, part(zn, 1)], Z1.at[slot, 0, pl.ds(32, 32)], s, rz1m_r.at[slot], up)
        send(SS.at[slot, part(zp_, 0)], Z1.at[slot, 1, pl.ds(0, 32)], s, rz1p_r.at[slot], down)

    def c3(h):
        slot = rem(h, DEP)
        s = ss_s.at[slot]
        done(Z2.at[slot, 0], rz2m_r.at[slot])
        b = part(zn, 0)
        SS[slot, b] = (SS[slot, b].astype(F32) + Z2[slot, 0].astype(F32)).astype(BF16)
        send(SS.at[slot, b], Z1.at[slot, 0, pl.ds(0, 32)], s, rz1m_r.at[slot], up)
        done(Z2.at[slot, 1], rz2p_r.at[slot])
        b = part(zp_, 1)
        SS[slot, b] = (SS[slot, b].astype(F32) + Z2[slot, 1].astype(F32)).astype(BF16)
        send(SS.at[slot, b], Z1.at[slot, 1, pl.ds(32, 32)], s, rz1p_r.at[slot], down)

    def c4(h):
        slot = rem(h, DEP)

        @pl.when(h >= DEP)
        def _():
            done(YS.at[slot], ys_s.at[slot])

        done(Z1.at[slot, 0], rz1m_r.at[slot])
        done(Z1.at[slot, 1], rz1p_r.at[slot])

        def total(yy):
            b = pl.ds(at16(yy * 32), 32)
            return SS[slot, part(z, yy)].astype(F32) + Z1[slot, 0, b].astype(F32) + Z1[slot, 1, b].astype(F32)

        YS[slot] = total(1 - yh).astype(BF16)
        send(YS.at[slot], YR.at[slot], ys_s.at[slot], yr_r.at[slot], across)
        TF[...] = total(yh)

    def c5(h):
        slot = rem(h, DEP)

        @pl.when(h >= DEP)
        def _():
            done(EB.at[slot, pl.ds(0, 336)], eb_s.at[slot])

        done(YR.at[slot], yr_r.at[slot])
        scale = jnp.where(h < NC, gslot[pl.ds(0, 32), :][:, :1], 1.0)
        v = ((TF[...] + YR[slot].astype(F32)) * scale).astype(BF16)
        v = jnp.concatenate([v[:, q * QW : (q + 1) * QW] for q in range(4)], axis=0)
        EB[slot] = dot(A[...], v).astype(BF16)
        for p in peers:
            send(EB.at[slot, pl.ds(at16(p * 48, 16), 48)], ER.at[slot, mine], eb_s.at[slot], er_r.at[slot], (dp, p))
        ER[slot, mine] = EB[slot, mine]

    def c6(h):
        slot = rem(h, DEP)
        done(ER.at[slot, pl.ds(0, 336)], er_r.at[slot])
        t = ER[slot, 0:48].astype(F32)
        for j in range(1, 8):
            t = t + ER[slot, 48 * j : 48 * j + 48].astype(F32)
        out_ref[h] = t.astype(BF16)

    def stage(f, i, n=2 * NC):
        @pl.when((i >= 0) & (i < n))
        def _():
            f(i)

    def step(t, carry):
        stage(a1, jnp.where(t + 2 < 2 * NC, t + 2, -1))
        stage(a2, t)
        stage(a4, t - LAG4)
        stage(a3, t)
        stage(a5, t - LAG5)
        stage(a6, t - LAG6)
        h = t - OFF
        stage(c6, h - L6)
        stage(c5, h - L5)
        stage(c4, h - L4)
        stage(c3, h - L3)
        stage(c2, h - L2)
        stage(c1, h)
        return carry

    lax.fori_loop(0, STEPS, step, 0)

    def finish(g, carry):
        done(G.at[g, pl.ds(0, 336)], ge_s.at[g])
        done(R.at[g, pl.ds(0, 480)], ag_s.at[g])
        pltpu.make_async_copy(R.at[g], rg_hbm.at[g], hbm_s.at[g]).wait()
        return carry

    lax.fori_loop(0, 2 * NC, finish, 0)
    for i in range(2):
        done(SB.at[i], sb_s.at[i])
    for i in range(DEP):
        done(SS.at[i, pl.ds(0, 192)], ss_s.at[i])
        done(YS.at[i], ys_s.at[i])
        done(EB.at[i, pl.ds(0, 336)], eb_s.at[i])


def grads(rows, slot_grad, hid, gp, gin, gout):
    gin[...] = dot(rows[0], gp[...], ((0,), (0,))).astype(BF16)
    gout[...] = dot(hid[...], slot_grad[0], ((0,), (0,))).astype(BF16)


def local(tokens, cotangent, expert_ids, gate_values, w_in, w_out):
    both = jnp.stack([tokens, cotangent])
    x = both.reshape(2, 12, NC, 4, QW).transpose(0, 2, 1, 3, 4).reshape(2 * NC, 48, QW)
    vmem, hbm = pl.BlockSpec(memory_space=pltpu.VMEM), pl.BlockSpec(memory_space=pl.ANY)
    dma = lambda n: pltpu.SemaphoreType.DMA((n,))
    out, rg, hid, gp = pl.pallas_call(
        exchange,
        name="exchange",
        out_shape=(
            jax.ShapeDtypeStruct((2 * NC, 48, QW), BF16),
            jax.ShapeDtypeStruct((2 * NC, ROWS, CW), BF16),
            jax.ShapeDtypeStruct((ROWS, HID), BF16),
            jax.ShapeDtypeStruct((ROWS, HID), BF16),
        ),
        in_specs=[vmem, vmem, vmem, hbm, hbm],
        out_specs=(vmem, hbm, vmem, vmem),
        scratch_shapes=[
            pltpu.VMEM((D, HID), BF16),
            pltpu.VMEM((HID, D), BF16),
            pltpu.VMEM((2 * NC, 4 * TOK, QW), BF16),
            pltpu.VMEM((2 * NC, ROWS, CW), BF16),
            pltpu.VMEM((ROWS, HID), F32),
            pltpu.VMEM((ROWS, HID), F32),
            pltpu.VMEM((4 * TOK, 128), BF16),
            pltpu.VMEM((4 * TOK, 128), F32),
            pltpu.VMEM((128, 128), F32),
            pltpu.VMEM((2, HALF, CW), BF16),
            pltpu.VMEM((HALF, CW), F32),
            pltpu.VMEM((DEP, HALF, CW), BF16),
            pltpu.VMEM((DEP, HALF, CW), BF16),
            pltpu.VMEM((DEP, 2, 32, CW), BF16),
            pltpu.VMEM((DEP, 2, 64, CW), BF16),
            pltpu.VMEM((DEP, 32, CW), BF16),
            pltpu.VMEM((DEP, 32, CW), BF16),
            pltpu.VMEM((32, CW), F32),
            pltpu.VMEM((DEP, 4 * TOK, QW), BF16),
            pltpu.VMEM((DEP, 4 * TOK, QW), BF16),
            dma(2),
        ]
        + [dma(2 * NC) for _ in range(10)]
        + [dma(2), dma(DEP), dma(DEP)]
        + [dma(DEP) for _ in range(8)],
        compiler_params=pltpu.CompilerParams(
            collective_id=0, has_side_effects=True, vmem_limit_bytes=56 * 2**20
        ),
    )(x, expert_ids, gate_values, w_in[0], w_out[0])
    one = lambda f: pl.BlockSpec((1, ROWS, CW), f)
    grad_in, grad_out = pl.pallas_call(
        grads,
        name="grads",
        grid=(NC,),
        out_shape=(
            jax.ShapeDtypeStruct((D, HID), BF16),
            jax.ShapeDtypeStruct((HID, D), BF16),
        ),
        in_specs=[
            one(lambda k: (k, 0, 0)),
            one(lambda k: (NC + k, 0, 0)),
            pl.BlockSpec((ROWS, HID), lambda k: (0, 0)),
            pl.BlockSpec((ROWS, HID), lambda k: (0, 0)),
        ],
        out_specs=(
            pl.BlockSpec((CW, HID), lambda k: (k, 0)),
            pl.BlockSpec((HID, CW), lambda k: (0, k)),
        ),
        compiler_params=pltpu.CompilerParams(vmem_limit_bytes=40 * 2**20),
    )(rg, rg, hid, gp)
    final = out.reshape(2, NC, 12, 4, QW).transpose(0, 2, 1, 3, 4).reshape(2, 12, D)
    return final[0], final[1], grad_in[None], grad_out[None]


def solution(mesh):
    placed = (
        P(("dp", "expert"), None),
        P(("dp", "expert"), None),
        P("dp", None),
        P("dp", None),
        P("expert", None, "dp"),
        P("expert", "dp", None),
    )
    return jax.shard_map(
        local,
        mesh=mesh,
        in_specs=placed,
        out_specs=(
            P(("dp", "expert"), None),
            P(("dp", "expert"), None),
            P("expert", None, "dp"),
            P("expert", "dp", None),
        ),
        check_vma=False,
    )
```

time: 591 us -> 189 us (0.32)
  waiting for transfers between devices: 413 us -> 0 us
  Pallas kernels: 0 us -> 173 us
  blocking collectives: 74.8 us -> 0 us
  matrix products: 61.3 us -> 0 us
  between operations: 14.9 us -> 0.69 us
  starting transfers between devices: 13.8 us -> 0 us
    reduce_scatter x2 -> x0, waiting for transfers between devices: 217 us -> none  [the longest x1 123 us: local(): lax.psum_scatter(jnp.einsum('rf,df->rd', piece, weight_in, preferred_elem...]
    all_gather x4 -> x0, waiting for transfers between devices: 193 us -> none  [the longest x1 63.9 us: local(): rows = lax.all_gather(packed, 'dp', axis=0, tiled=True)]
    pallas_call x0 -> x2, Pallas kernels: none -> 173 us  [the longest x1 165 us: local(): pl.pallas_call(exchange, name='exchange', out_shape=(jax.ShapeDtypeStruct...]
    unnamed x1 -> x0, blocking collectives: 74.8 us -> none
    dot_general x10 -> x0, matrix products: 61.3 us -> none  [the longest x1 11 us: local(): jnp.einsum('rf,df->rd', piece, weight_in, preferred_element_type=jnp.floa...]
    unnamed x4 -> x0, starting transfers between devices: 13.4 us -> none
  transfers between devices with their start and end apart: 10 -> 0, of which waited for: 7 -> 0; matrix products, arithmetic and copies ran while one was open for 11% -> 0% of each run, Pallas kernels for 0% -> 0%
where the time goes in v1:
time: 189 us; the launch traced here: 188 us
  Pallas kernels  173 us (92%)
  local copies, waits for them, and re-layouts  14.1 us (7%)
    pallas_call x1, Pallas kernels, local(): pl.pallas_call(exchange, name='exchange', out_shape=(jax.ShapeDtypeStruct...  165 us
    unnamed x10, local copies, waits for them, and re-layouts  9.44 us
    pallas_call x1, Pallas kernels, local(): pl.pallas_call(grads, name='grads', grid=(NC,), out_shape=(jax.ShapeDtype...  8.77 us

profile of v1, /device:TPU:0, one launch (start us, length us, event | category | flops | bytes accessed | tf_op | source)
XLA Modules:
  0.0 188.3 jit_solution(5391619391335387784)
XLA Ops:
  0.6 1.0 stack.10
  1.6 1.0 stack.9
  2.7 0.1 copy_bitcast_fusion
  2.8 0.8 reshape.24.x_ref
  3.6 1.4 copy.12.ids_ref
  5.0 1.4 copy.13.gates_ref
  6.4 164.6 %exchange.1 = (bf16[12,48,256]{2,1,0:T(8,128)(2,1)}, bf16[12,512,1024]{2,1,0:T(8,128)(2,1)}, bf16[512,512]{1,0:T(8,128)(2,1)}, bf16[512,512]{1,0:T(8,128)(2,1)}) custom-call(bf16[12,48,256]{2,1,0:T(8,128)(2,1)} %reshape.24.x_ref, s32[96,2]{1,0:T(8,128)} %copy.12.ids_ref, f32[96,2]{1,0:T(8,128)} %copy.13.gates_ref, bf16[6144,512]{1,0:T(8,128)(2,1)} %bitcast.7, ...), custom_call_target="tpu_custom_call" | custom-call | tf_op jit(solution)/shard_map/exchange/pallas_call | solution.py:326
  171.0 0.0 copy-start
  171.0 4.6 %copy-done = bf16[12,512,1024]{2,1,0:T(8,128)(2,1)S(1)} copy-done((bf16[12,512,1024]{2,1,0:T(8,128)(2,1)S(1)}, bf16[12,512,1024]{2,1,0:T(8,128)(2,1)}, u32[]{:S(2)}) %copy-start) | copy-done | bytes 12582936
  175.6 0.0 copy-start.1
  175.6 1.0 copy-done.1
  176.6 0.0 copy-start.2
  176.6 1.0 copy-done.2
  177.7 0.0 copy-start.3
  177.7 8.8 %grads.1 = (bf16[6144,512]{1,0:T(8,128)(2,1)}, bf16[512,6144]{1,0:T(8,128)(2,1)}) custom-call(bf16[12,512,1024]{2,1,0:T(8,128)(2,1)S(1)} %copy-done, bf16[12,512,1024]{2,1,0:T(8,128)(2,1)S(1)} %copy-done, bf16[512,512]{1,0:T(8,128)(2,1)S(1)} %copy-done.1, bf16[512,512]{1,0:T(8,128)(2,1)S(1)} %copy-done.2), custom_call_target="tpu_custom_call" | custom-call | tf_op jit(solution)/shard_map/grads/pallas_call | solution.py:368
  186.5 0.0 copy-done.3
  186.5 0.1 reshape.25
  186.5 0.1 fusion
  186.7 0.1 copy.14
  186.7 0.8 squeeze.14
  187.5 0.1 copy.15
  187.5 0.8 squeeze.15
Async XLA Ops:
  171.0 4.6 %copy-start = (bf16[12,512,1024]{2,1,0:T(8,128)(2,1)S(1)}, bf16[12,512,1024]{2,1,0:T(8,128)(2,1)}, u32[]{:S(2)}) copy-start(bf16[12,512,1024]{2,1,0:T(8,128)(2,1)} %get-tuple-element.11.rows.slot_grad) | copy-start | bytes 37748740
  175.6 1.0 copy-start.1
  176.6 1.0 copy-start.2
  177.7 8.8 %copy-start.3 = (bf16[12,48,256]{2,1,0:T(8,128)(2,1)S(1)}, bf16[12,48,256]{2,1,0:T(8,128)(2,1)}, u32[]{:S(2)}) copy-start(bf16[12,48,256]{2,1,0:T(8,128)(2,1)} %get-tuple-element.10) | copy-start | bytes 884740

commit v2 on v1

v2 whole, which is shorter than its diff:
```python
import functools
import jax
import jax.numpy as jnp
from jax import lax
from jax.experimental import pallas as pl
from jax.experimental.pallas import tpu as pltpu
from jax.sharding import PartitionSpec as P

D = 6144
HID = 512
CAP = 32
TOK = 96
NC = 6
CW = D // NC
QW = CW // 4
ROWS = 512
HALF = 256
DEP = 6
MOD, WHICH = 3, 2
LEAD = 3
LAG3, LAG4, LAG5, LAGY, LAG6 = 1, 3, 5, 6, 7
OFF = NC + LAG6
L2, L3, L4, L5, L6, L7 = 1, 3, 5, 7, 9, 11
STEPS = OFF + 2 * NC + L7
MESH = pl.DeviceIdType.MESH
F32, BF16 = jnp.float32, jnp.bfloat16


def rem(a, b):
    return lax.rem(a, jnp.int32(b))


def at16(v, m=32):
    return pl.multiple_of(v, m)


def dot(a, b, dims=((1,), (0,)), precision=None):
    return lax.dot_general(a, b, (dims, ((), ())), precision=precision, preferred_element_type=F32)


def y_first(i):
    return i % MOD == WHICH if isinstance(i, int) else rem(i, MOD) == WHICH


def done(ref, sem):
    pltpu.make_async_copy(ref, ref, sem).wait()


def exchange(
    tok_ref, cot_ref, ids_ref, gates_ref, win_hbm, wout_hbm,
    lo_ref, gt_ref, rg_hbm, hid, gp,
    win, wout, X, G, R, pre, gh, A, grep, gslot,
    SB, PO, RB, SS, Z2, Z1, YB, YS, YR, TF, EB, ER, FB, FR, FT,
    w_sem, ge_s, ge_r, gp_r, ag_s, y_r, zm_r, zp_r, z2m_r, z2p_r, sib_r, hbm_s,
    sb_s, rb_r, ss_s, ry_r, rz2m_r, rz2p_r, rz1m_r, rz1p_r, ys_s, yr_r, eb_s, er_r, fb_s, fr_r,
):
    dp, e = lax.axis_index("dp"), lax.axis_index("expert")
    z, yh, c = dp // 4, (dp // 2) % 2, dp % 2
    yl, x = e // 4, e % 4

    def at(zz, yy, cc):
        return (zz * 4 + yy * 2 + cc, e)

    zn, zp_, zo = rem(z + 1, 4), rem(z + 3, 4), rem(z + 2, 4)
    up, down, across, sib = at(zn, yh, c), at(zp_, yh, c), at(z, 1 - yh, c), at(z, yh, 1 - c)
    xs = [rem(x + d, 4) for d in range(1, 4)]
    peers = [(dp, yl * 4 + p) for p in xs]
    pair = (dp, (1 - yl) * 4 + x)

    def send(src, dst, ss, rs, to):
        pltpu.make_async_remote_copy(
            src_ref=src, dst_ref=dst, send_sem=ss, recv_sem=rs, device_id=to, device_id_type=MESH
        ).start()

    load_in = pltpu.make_async_copy(win_hbm, win, w_sem.at[0])
    load_out = pltpu.make_async_copy(wout_hbm, wout, w_sem.at[1])
    load_in.start()
    load_out.start()

    barrier = pltpu.get_barrier_semaphore()
    for to in [up, down, across, sib, pair] + peers:
        pl.semaphore_signal(barrier, inc=1, device_id=to, device_id_type=MESH)
    pl.semaphore_wait(barrier, 8)

    mine = pl.ds(at16((x * 2 + yl) * 48, 16), 48)
    twin = pl.ds(at16((x * 2 + 1 - yl) * 48, 16), 48)

    def quarters(v):
        return jnp.concatenate([v[:, q * QW : (q + 1) * QW] for q in range(4)], axis=0)

    def a1(g):
        k = jnp.where(g < NC, g, g - NC)
        where = pl.ds(at16(k * CW, CW), CW)
        v = jnp.where(g < NC, tok_ref[:, where].astype(F32), cot_ref[:, where].astype(F32))
        v = quarters(v).astype(BF16)
        X[g] = v
        G[g, mine] = v
        send(X.at[g], G.at[g, mine], ge_s.at[g], gp_r.at[g], pair)
        for to in peers:
            send(X.at[g], G.at[g, mine], ge_s.at[g], ge_r.at[g], to)

    def a1b(g):
        b = G.at[g, twin]
        done(b, gp_r.at[g])
        for to in peers:
            send(b, b, ge_s.at[g], ge_r.at[g], to)

    for g in range(LEAD):
        a1(jnp.int32(g))

    chosen = ids_ref[...] == e
    gsum = jnp.sum(jnp.where(chosen, gates_ref[...], 0.0), axis=0, keepdims=True)
    picked = jnp.max(jnp.where(chosen, 1.0, 0.0), axis=0, keepdims=True)
    row = lax.broadcasted_iota(jnp.int32, (TOK, TOK), 0)
    col = lax.broadcasted_iota(jnp.int32, (TOK, TOK), 1)
    tri = jnp.where(row <= col, 1.0, 0.0).astype(BF16)
    pickb = jnp.broadcast_to(picked, (128, TOK))
    place = dot(pickb.astype(BF16), tri) - 1.0
    slots = jnp.bitwise_and(lax.broadcasted_iota(jnp.int32, (128, TOK), 0), 31).astype(F32)
    table = jnp.where(place == slots, pickb, 0.0)
    r4 = lax.broadcasted_iota(jnp.int32, (4 * TOK, 128), 0)
    c4_ = lax.broadcasted_iota(jnp.int32, (4 * TOK, 128), 1)
    j4 = jnp.right_shift(r4 * 683, 15)
    rest = r4 - j4 * 48
    q_r = jnp.right_shift(rest * 171, 11)
    token = (jnp.bitwise_and(j4, 1) * 4 + jnp.right_shift(j4, 1)) * 12 + rest - q_r * 12
    q_c = jnp.right_shift(c4_, 5)
    widen = jnp.where(token == c4_, 1.0, 0.0)[:, :TOK]
    nt = ((1,), (1,))
    wide = dot(widen.astype(BF16), table.astype(BF16), nt)
    A[...] = jnp.where(q_r == q_c, wide, 0.0).astype(BF16)
    gsb = jnp.broadcast_to(gsum, (128, TOK))
    grep[...] = dot(widen, gsb, nt, lax.Precision.HIGHEST)
    gslot[...] = dot(table, gsb, nt, lax.Precision.HIGHEST)

    a1b(jnp.int32(0))

    pre[...] = jnp.zeros_like(pre)
    gh[...] = jnp.zeros_like(gh)

    def block(zz, yy, n=32, skip=0):
        return pl.ds(at16((c * 8 + yy * 4 + zz) * 32 + skip, 16), n)

    def to_sib(g, where):
        send(R.at[g, where], R.at[g, where], ag_s.at[g], sib_r.at[g], sib)

    def a2(g):
        done(G.at[g, pl.ds(0, 288)], ge_r.at[g])
        scale = jnp.where(g < NC, 1.0, grep[...][:, :1])
        v = (G[g].astype(F32) * scale).astype(BF16)
        packed = dot(A[...], v, ((0,), (0,))).astype(BF16)
        own = block(z, yh)
        for q in range(4):
            R[g, own, q * QW : (q + 1) * QW] = packed[q * 32 : (q + 1) * 32]
        me = R.at[g, own]
        send(me, me, ag_s.at[g], y_r.at[g], across)
        send(me, me, ag_s.at[g], zm_r.at[g], up)
        send(me, me, ag_s.at[g], zp_r.at[g], down)
        to_sib(g, own)

    def a3(g):
        @pl.when(jnp.logical_not(y_first(g)))
        def _():
            theirs = block(z, 1 - yh)
            b = R.at[g, theirs]
            done(b, y_r.at[g])
            send(b, b, ag_s.at[g], zm_r.at[g], up)
            send(b, b, ag_s.at[g], zp_r.at[g], down)
            to_sib(g, theirs)

    def a4(g):
        def hand_on(zz, sem, sem2, to, pick):
            @pl.when(jnp.logical_not(y_first(g)))
            def _():
                done(R.at[g, pl.ds(0, 64)], sem.at[g])
                b = R.at[g, block(zz, pick)]
                send(b, b, ag_s.at[g], sem2.at[g], to)
                to_sib(g, block(zz, 0))
                to_sib(g, block(zz, 1))

            @pl.when(y_first(g))
            def _():
                whole = R.at[g, block(zz, yh)]
                done(whole, sem.at[g])
                b = R.at[g, block(zz, yh, 16, 16 * pick)]
                send(b, b, ag_s.at[g], sem2.at[g], to)
                send(whole, whole, ag_s.at[g], y_r.at[g], across)
                to_sib(g, block(zz, yh))

        hand_on(zp_, zm_r, z2m_r, up, 0)
        hand_on(zn, zp_r, z2p_r, down, 1)

    def a5(g):
        @pl.when(jnp.logical_not(y_first(g)))
        def _():
            done(R.at[g, block(zo, 0)], z2m_r.at[g])
            done(R.at[g, block(zo, 1)], z2p_r.at[g])
            to_sib(g, block(zo, 0))
            to_sib(g, block(zo, 1))

        @pl.when(y_first(g))
        def _():
            done(R.at[g, block(zo, yh, 16)], z2m_r.at[g])
            done(R.at[g, block(zo, yh, 16, 16)], z2p_r.at[g])
            b = R.at[g, block(zo, yh)]
            send(b, b, ag_s.at[g], y_r.at[g], across)
            to_sib(g, block(zo, yh))

    def ay(g):
        @pl.when(y_first(g))
        def _():
            b = block(0, 1 - yh, 128)
            done(R.at[g, b], y_r.at[g])
            to_sib(g, b)

    def a6(g):
        done(R.at[g, pl.ds(at16((1 - c) * HALF), HALF)], sib_r.at[g])
        pltpu.make_async_copy(R.at[g], rg_hbm.at[g], hbm_s.at[g]).start()

        @pl.when(g == 0)
        def _():
            load_in.wait()
            load_out.wait()

        @pl.when(g < NC)
        def _():
            pre[...] += dot(R[g], win[pl.ds(at16(g * CW, CW), CW), :])

        @pl.when(g >= NC)
        def _():
            gh[...] += dot(R[g], wout[:, pl.ds(at16((g - NC) * CW, CW), CW)], ((1,), (1,)))

        @pl.when(g == NC - 1)
        def _():
            v = pre[...]
            hid[...] = (v * jax.nn.sigmoid(v)).astype(BF16)

        @pl.when(g == 2 * NC - 1)
        def _():
            v = pre[...]
            s = jax.nn.sigmoid(v)
            gp[...] = (gh[...] * s * (1.0 + v * (1.0 - s))).astype(BF16)

    ours, others = pl.ds(at16(c * HALF), HALF), pl.ds(at16((1 - c) * HALF), HALF)

    def c1(h):
        two, slot = rem(h, 2), rem(h, DEP)

        @pl.when(h >= 2)
        def _():
            done(SB.at[two], sb_s.at[two])

        def product(lhs, w, dims):
            SB[two] = dot(lhs[others, :], w, dims).astype(BF16)
            send(SB.at[two], RB.at[slot], sb_s.at[two], rb_r.at[slot], sib)
            PO[...] = dot(lhs[ours, :], w, dims)

        @pl.when(h < NC)
        def _():
            product(hid, wout[:, pl.ds(at16(h * CW, CW), CW)], ((1,), (0,)))

        @pl.when(h >= NC)
        def _():
            product(gp, win[pl.ds(at16((h - NC) * CW, CW), CW), :], ((1,), (1,)))

    def part(zz, yy, n=32, skip=0):
        return pl.ds(at16((yy * 4 + zz) * 32 + skip, 16), n)

    def either(h, z_way, y_way):
        pl.when(jnp.logical_not(y_first(h)))(z_way)
        pl.when(y_first(h))(y_way)

    def sent(slot, i):
        either(
            i,
            lambda: done(SS.at[slot, pl.ds(0, 192)], ss_s.at[slot]),
            lambda: done(SS.at[slot, pl.ds(0, 224)], ss_s.at[slot]),
        )

    def add_into(slot, b, v):
        SS[slot, b] = (SS[slot, b].astype(F32) + v.astype(F32)).astype(BF16)

    def c2(h):
        slot = rem(h, DEP)

        @pl.when(h >= DEP)
        def _():
            sent(slot, h - DEP)

        done(RB.at[slot], rb_r.at[slot])
        SS[slot] = (PO[...] + RB[slot].astype(F32)).astype(BF16)
        s = ss_s.at[slot]

        def z_way():
            send(SS.at[slot, part(zo, 0)], Z2.at[slot, 0], s, rz2m_r.at[slot], up)
            send(SS.at[slot, part(zo, 1)], Z2.at[slot, 1], s, rz2p_r.at[slot], down)
            send(SS.at[slot, part(zn, 1)], Z1.at[slot, 0, pl.ds(32, 32)], s, rz1m_r.at[slot], up)
            send(SS.at[slot, part(zp_, 0)], Z1.at[slot, 1, pl.ds(0, 32)], s, rz1p_r.at[slot], down)

        def y_way():
            send(SS.at[slot, part(0, 1 - yh, 128)], YB.at[slot], s, ry_r.at[slot], across)

        either(h, z_way, y_way)

    def c3(h):
        slot = rem(h, DEP)
        s = ss_s.at[slot]

        def z_way():
            done(Z2.at[slot, 0], rz2m_r.at[slot])
            b = part(zn, 0)
            add_into(slot, b, Z2[slot, 0])
            send(SS.at[slot, b], Z1.at[slot, 0, pl.ds(0, 32)], s, rz1m_r.at[slot], up)
            done(Z2.at[slot, 1], rz2p_r.at[slot])
            b = part(zp_, 1)
            add_into(slot, b, Z2[slot, 1])
            send(SS.at[slot, b], Z1.at[slot, 1, pl.ds(32, 32)], s, rz1p_r.at[slot], down)

        def y_way():
            done(YB.at[slot], ry_r.at[slot])
            add_into(slot, part(0, yh, 128), YB[slot])
            send(SS.at[slot, part(zo, yh, 16)], Z2.at[slot, 0, pl.ds(0, 16)], s, rz2m_r.at[slot], up)
            send(SS.at[slot, part(zo, yh, 16, 16)], Z2.at[slot, 1, pl.ds(0, 16)], s, rz2p_r.at[slot], down)
            send(SS.at[slot, part(zn, yh, 16, 16)], Z1.at[slot, 0, pl.ds(16, 16)], s, rz1m_r.at[slot], up)
            send(SS.at[slot, part(zp_, yh, 16)], Z1.at[slot, 1, pl.ds(0, 16)], s, rz1p_r.at[slot], down)

        either(h, z_way, y_way)

    def c4(h):
        slot = rem(h, DEP)
        s = ss_s.at[slot]

        @pl.when((h >= DEP) & jnp.logical_not(y_first(h - DEP)))
        def _():
            done(YS.at[slot], ys_s.at[slot])

        def z_way():
            done(Z1.at[slot, 0], rz1m_r.at[slot])
            done(Z1.at[slot, 1], rz1p_r.at[slot])

            def total(yy):
                b = pl.ds(at16(yy * 32), 32)
                return SS[slot, part(z, yy)].astype(F32) + Z1[slot, 0, b].astype(F32) + Z1[slot, 1, b].astype(F32)

            YS[slot] = total(1 - yh).astype(BF16)
            send(YS.at[slot], YR.at[slot], ys_s.at[slot], yr_r.at[slot], across)
            TF[slot] = total(yh)

        def y_way():
            done(Z2.at[slot, 0, pl.ds(0, 16)], rz2m_r.at[slot])
            b = part(zn, yh, 16)
            add_into(slot, b, Z2[slot, 0, 0:16])
            send(SS.at[slot, b], Z1.at[slot, 0, pl.ds(0, 16)], s, rz1m_r.at[slot], up)
            done(Z2.at[slot, 1, pl.ds(0, 16)], rz2p_r.at[slot])
            b = part(zp_, yh, 16, 16)
            add_into(slot, b, Z2[slot, 1, 0:16])
            send(SS.at[slot, b], Z1.at[slot, 1, pl.ds(16, 16)], s, rz1p_r.at[slot], down)

        either(h, z_way, y_way)

    def c5(h):
        slot = rem(h, DEP)

        @pl.when(h >= DEP)
        def _():
            done(EB.at[slot, pl.ds(0, 288)], eb_s.at[slot])

        def z_way():
            done(YR.at[slot], yr_r.at[slot])
            TF[slot] += YR[slot].astype(F32)

        def y_way():
            done(Z1.at[slot, 0, pl.ds(0, 32)], rz1m_r.at[slot])
            done(Z1.at[slot, 1, pl.ds(0, 32)], rz1p_r.at[slot])
            TF[slot] = SS[slot, part(z, yh)].astype(F32) + Z1[slot, 0, 0:32].astype(F32) + Z1[slot, 1, 0:32].astype(F32)

        either(h, z_way, y_way)
        scale = jnp.where(h < NC, gslot[pl.ds(0, 32), :][:, :1], 1.0)
        EB[slot] = dot(A[...], quarters((TF[slot] * scale).astype(BF16))).astype(BF16)
        here = pl.ds(at16(x * 96), 96)
        for p, to in zip(xs, peers):
            send(EB.at[slot, pl.ds(at16(p * 96), 96)], ER.at[slot, here], eb_s.at[slot], er_r.at[slot], to)
        ER[slot, here] = EB[slot, here]

    def c6(h):
        slot = rem(h, DEP)

        @pl.when(h >= DEP)
        def _():
            done(FB.at[slot], fb_s.at[slot])

        done(ER.at[slot, pl.ds(0, 288)], er_r.at[slot])

        def total(yy):
            t = ER[slot, pl.ds(at16(yy * 48, 16), 48)].astype(F32)
            for j in range(1, 4):
                t = t + ER[slot, pl.ds(at16(96 * j + yy * 48, 16), 48)].astype(F32)
            return t

        FB[slot] = total(1 - yl).astype(BF16)
        send(FB.at[slot], FR.at[slot], fb_s.at[slot], fr_r.at[slot], pair)
        FT[slot] = total(yl)

    def c7(h):
        slot = rem(h, DEP)
        done(FR.at[slot], fr_r.at[slot])
        t = FT[slot] + FR[slot].astype(F32)
        t = jnp.concatenate([t[12 * q : 12 * q + 12] for q in range(4)], axis=1).astype(BF16)

        @pl.when(h < NC)
        def _():
            lo_ref[:, pl.ds(at16(h * CW, CW), CW)] = t

        @pl.when(h >= NC)
        def _():
            gt_ref[:, pl.ds(at16((h - NC) * CW, CW), CW)] = t

    def stage(f, i, n=2 * NC):
        @pl.when((i >= 0) & (i < n))
        def _():
            f(i)

    def step(t, carry):
        stage(a1, t + LEAD)
        stage(a2, t)
        stage(a1b, t + 1)
        stage(a3, t - LAG3)
        stage(a4, t - LAG4)
        stage(a5, t - LAG5)
        stage(ay, t - LAGY)
        stage(a6, t - LAG6)
        h = t - OFF
        stage(c7, h - L7)
        stage(c6, h - L6)
        stage(c5, h - L5)
        stage(c4, h - L4)
        stage(c3, h - L3)
        stage(c2, h - L2)
        stage(c1, h)
        return carry

    lax.fori_loop(0, STEPS, step, 0)

    def finish(g, carry):
        done(G.at[g, pl.ds(0, 336)], ge_s.at[g])
        done(R.at[g, pl.ds(0, 480)], ag_s.at[g])
        pltpu.make_async_copy(R.at[g], rg_hbm.at[g], hbm_s.at[g]).wait()
        return carry

    lax.fori_loop(0, 2 * NC, finish, 0)
    for i in range(2):
        done(SB.at[i], sb_s.at[i])
    for i in range(2 * NC - DEP, 2 * NC):
        slot = i % DEP
        if y_first(i):
            done(SS.at[slot, pl.ds(0, 224)], ss_s.at[slot])
        else:
            done(SS.at[slot, pl.ds(0, 192)], ss_s.at[slot])
            done(YS.at[slot], ys_s.at[slot])
        done(EB.at[slot, pl.ds(0, 288)], eb_s.at[slot])
        done(FB.at[slot], fb_s.at[slot])


def grads(rows, slot_grad, hid, gp, gin, gout):
    gin[...] = dot(rows[0], gp[...], ((0,), (0,))).astype(BF16)
    gout[...] = dot(hid[...], slot_grad[0], ((0,), (0,))).astype(BF16)


def local(tokens, cotangent, expert_ids, gate_values, w_in, w_out):
    vmem, hbm = pl.BlockSpec(memory_space=pltpu.VMEM), pl.BlockSpec(memory_space=pl.ANY)
    dma = lambda n: pltpu.SemaphoreType.DMA((n,))
    layer_out, grad_tokens, rg, hid, gp = pl.pallas_call(
        exchange,
        name="exchange",
        out_shape=(
            jax.ShapeDtypeStruct((12, D), BF16),
            jax.ShapeDtypeStruct((12, D), BF16),
            jax.ShapeDtypeStruct((2 * NC, ROWS, CW), BF16),
            jax.ShapeDtypeStruct((ROWS, HID), BF16),
            jax.ShapeDtypeStruct((ROWS, HID), BF16),
        ),
        in_specs=[vmem, vmem, vmem, vmem, hbm, hbm],
        out_specs=(vmem, vmem, hbm, vmem, vmem),
        scratch_shapes=[
            pltpu.VMEM((D, HID), BF16),
            pltpu.VMEM((HID, D), BF16),
            pltpu.VMEM((2 * NC, 48, QW), BF16),
            pltpu.VMEM((2 * NC, 4 * TOK, QW), BF16),
            pltpu.VMEM((2 * NC, ROWS, CW), BF16),
            pltpu.VMEM((ROWS, HID), F32),
            pltpu.VMEM((ROWS, HID), F32),
            pltpu.VMEM((4 * TOK, 128), BF16),
            pltpu.VMEM((4 * TOK, 128), F32),
            pltpu.VMEM((128, 128), F32),
            pltpu.VMEM((2, HALF, CW), BF16),
            pltpu.VMEM((HALF, CW), F32),
            pltpu.VMEM((DEP, HALF, CW), BF16),
            pltpu.VMEM((DEP, HALF, CW), BF16),
            pltpu.VMEM((DEP, 2, 32, CW), BF16),
            pltpu.VMEM((DEP, 2, 64, CW), BF16),
            pltpu.VMEM((DEP, 128, CW), BF16),
            pltpu.VMEM((DEP, 32, CW), BF16),
            pltpu.VMEM((DEP, 32, CW), BF16),
            pltpu.VMEM((DEP, 32, CW), F32),
            pltpu.VMEM((DEP, 4 * TOK, QW), BF16),
            pltpu.VMEM((DEP, 4 * TOK, QW), BF16),
            pltpu.VMEM((DEP, 48, QW), BF16),
            pltpu.VMEM((DEP, 48, QW), BF16),
            pltpu.VMEM((DEP, 48, QW), F32),
            dma(2),
        ]
        + [dma(2 * NC) for _ in range(11)]
        + [dma(2), dma(DEP), dma(DEP)]
        + [dma(DEP) for _ in range(11)],
        compiler_params=pltpu.CompilerParams(
            collective_id=0, has_side_effects=True, vmem_limit_bytes=56 * 2**20
        ),
    )(tokens, cotangent, expert_ids.T, gate_values.T, w_in[0], w_out[0])
    one = lambda f: pl.BlockSpec((1, ROWS, CW), f)
    grad_in, grad_out = pl.pallas_call(
        grads,
        name="grads",
        grid=(NC,),
        out_shape=(
            jax.ShapeDtypeStruct((D, HID), BF16),
            jax.ShapeDtypeStruct((HID, D), BF16),
        ),
        in_specs=[
            one(lambda k: (k, 0, 0)),
            one(lambda k: (NC + k, 0, 0)),
            pl.BlockSpec((ROWS, HID), lambda k: (0, 0)),
            pl.BlockSpec((ROWS, HID), lambda k: (0, 0)),
        ],
        out_specs=(
            pl.BlockSpec((CW, HID), lambda k: (k, 0)),
            pl.BlockSpec((HID, CW), lambda k: (0, k)),
        ),
        compiler_params=pltpu.CompilerParams(vmem_limit_bytes=62 * 2**20),
    )(rg, rg, hid, gp)
    return layer_out, grad_tokens, grad_in[None], grad_out[None]


def solution(mesh):
    placed = (
        P(("dp", "expert"), None),
        P(("dp", "expert"), None),
        P("dp", None),
        P("dp", None),
        P("expert", None, "dp"),
        P("expert", "dp", None),
    )
    return jax.shard_map(
        local,
        mesh=mesh,
        in_specs=placed,
        out_specs=(
            P(("dp", "expert"), None),
            P(("dp", "expert"), None),
            P("expert", None, "dp"),
            P("expert", "dp", None),
        ),
        check_vma=False,
    )
```

time: 189 us -> 155 us (0.82)
  Pallas kernels: 173 us -> 152 us
  local copies, waits for them, and re-layouts: 14.1 us -> 1.36 us
    pallas_call x1, Pallas kernels: 165 us -> 139 us  [local(): pl.pallas_call(exchange, name='exchange', out_shape=(jax.ShapeDtypeStruct...]
    unnamed x10 -> x6, local copies, waits for them, and re-layouts: 9.44 us -> 1.36 us
    pallas_call x1, Pallas kernels: 8.77 us -> 13 us  [local(): pl.pallas_call(grads, name='grads', grid=(NC,), out_shape=(jax.ShapeDtype...]
    another operation x2 -> x0, local copies, waits for them, and re-layouts: 2.03 us -> none  [local(): both = jnp.stack([tokens, cotangent])]
where the time goes in v2:
time: 155 us; the launch traced here: 154 us
  Pallas kernels  152 us (98%)
    pallas_call x1, Pallas kernels, local(): pl.pallas_call(exchange, name='exchange', out_shape=(jax.ShapeDtypeStruct...  139 us
    pallas_call x1, Pallas kernels, local(): pl.pallas_call(grads, name='grads', grid=(NC,), out_shape=(jax.ShapeDtype...  13 us

profile of v2, /device:TPU:0, one launch (start us, length us, event | category | flops | bytes accessed | tf_op | source)
XLA Modules:
  0.0 154.4 jit_solution(17849268251941393152)
XLA Ops:
  0.6 139.3 %exchange.1 = (bf16[12,6144]{1,0:T(8,128)(2,1)}, bf16[12,6144]{1,0:T(8,128)(2,1)}, bf16[12,512,1024]{2,1,0:T(8,128)(2,1)}, bf16[512,512]{1,0:T(8,128)(2,1)}, bf16[512,512]{1,0:T(8,128)(2,1)}) custom-call(bf16[12,6144]{1,0:T(8,128)(2,1)} %tok_ref.1, bf16[12,6144]{1,0:T(8,128)(2,1)} %cot_ref.1, s32[2,96]{1,0:T(2,128)} %bitcast.8, f32[2,96]{1,0:T(2,128)} %bitcast.9, ...), custom_call_target="tpu_custom_call" | custom-call | tf_op jit(solution)/shard_map/exchange/pallas_call | solution.py:472
  139.9 0.0 copy-start.1
  139.9 0.0 copy-start
  140.0 13.0 %grads.1 = (bf16[6144,512]{1,0:T(8,128)(2,1)}, bf16[512,6144]{1,0:T(8,128)(2,1)}) custom-call(bf16[12,512,1024]{2,1,0:T(8,128)(2,1)} %get-tuple-element.13.rows.slot_grad, bf16[12,512,1024]{2,1,0:T(8,128)(2,1)} %get-tuple-element.13.rows.slot_grad, bf16[512,512]{1,0:T(8,128)(2,1)} %get-tuple-element.14.hid, bf16[512,512]{1,0:T(8,128)(2,1)} %get-tuple-element.15.gp), custom_call_target="tpu_custom_call" | custom-call | tf_op jit(solution)/shard_map/grads/pallas_call | solution.py:520
  153.0 0.0 copy-done.1
  153.0 0.7 copy.12
  153.7 0.0 copy-done
  153.7 0.7 copy.13
Async XLA Ops:
  139.9 13.1 %copy-start.1 = (bf16[12,6144]{1,0:T(8,128)(2,1)S(1)}, bf16[12,6144]{1,0:T(8,128)(2,1)}, u32[]{:S(2)}) copy-start(bf16[12,6144]{1,0:T(8,128)(2,1)} %get-tuple-element.22) | copy-start | bytes 442372
  139.9 13.7 %copy-start = (bf16[12,6144]{1,0:T(8,128)(2,1)S(1)}, bf16[12,6144]{1,0:T(8,128)(2,1)}, u32[]{:S(2)}) copy-start(bf16[12,6144]{1,0:T(8,128)(2,1)} %get-tuple-element.23) | copy-start | bytes 442372

commit v3 on v2

--- a/solution.py
+++ b/solution.py
@@ -48,8 +48,8 @@
 
 def exchange(
     tok_ref, cot_ref, ids_ref, gates_ref, win_hbm, wout_hbm,
-    lo_ref, gt_ref, rg_hbm, hid, gp,
-    win, wout, X, G, R, pre, gh, A, grep, gslot,
+    lo_ref, gt_ref, rt_hbm, sg_hbm, hidt, gp,
+    win, wout, X, G, R, RT, hid, pre, gh, A, AT, grep, gslot,
     SB, PO, RB, SS, Z2, Z1, YB, YS, YR, TF, EB, ER, FB, FR, FT,
     w_sem, ge_s, ge_r, gp_r, ag_s, y_r, zm_r, zp_r, z2m_r, z2p_r, sib_r, hbm_s,
     sb_s, rb_r, ss_s, ry_r, rz2m_r, rz2p_r, rz1m_r, rz1p_r, ys_s, yr_r, eb_s, er_r, fb_s, fr_r,
@@ -65,6 +65,7 @@
     up, down, across, sib = at(zn, yh, c), at(zp_, yh, c), at(z, 1 - yh, c), at(z, yh, 1 - c)
     xs = [rem(x + d, 4) for d in range(1, 4)]
     peers = [(dp, yl * 4 + p) for p in xs]
+    far = [(dp, (1 - yl) * 4 + p) for p in xs]
     pair = (dp, (1 - yl) * 4 + x)
 
     def send(src, dst, ss, rs, to):
@@ -78,9 +79,9 @@
     load_out.start()
 
     barrier = pltpu.get_barrier_semaphore()
-    for to in [up, down, across, sib, pair] + peers:
+    for to in [up, down, across, sib, pair] + peers + far:
         pl.semaphore_signal(barrier, inc=1, device_id=to, device_id_type=MESH)
-    pl.semaphore_wait(barrier, 8)
+    pl.semaphore_wait(barrier, 11)
 
     mine = pl.ds(at16((x * 2 + yl) * 48, 16), 48)
     twin = pl.ds(at16((x * 2 + 1 - yl) * 48, 16), 48)
@@ -88,7 +89,7 @@
     def quarters(v):
         return jnp.concatenate([v[:, q * QW : (q + 1) * QW] for q in range(4)], axis=0)
 
-    def a1(g):
+    def a1(g, reach=()):
         k = jnp.where(g < NC, g, g - NC)
         where = pl.ds(at16(k * CW, CW), CW)
         v = jnp.where(g < NC, tok_ref[:, where].astype(F32), cot_ref[:, where].astype(F32))
@@ -96,7 +97,7 @@
         X[g] = v
         G[g, mine] = v
         send(X.at[g], G.at[g, mine], ge_s.at[g], gp_r.at[g], pair)
-        for to in peers:
+        for to in [*peers, *reach]:
             send(X.at[g], G.at[g, mine], ge_s.at[g], ge_r.at[g], to)
 
     def a1b(g):
@@ -105,7 +106,8 @@
         for to in peers:
             send(b, b, ge_s.at[g], ge_r.at[g], to)
 
-    for g in range(LEAD):
+    a1(jnp.int32(0), far)
+    for g in range(1, LEAD):
         a1(jnp.int32(g))
 
     chosen = ids_ref[...] == e
@@ -128,12 +130,15 @@
     widen = jnp.where(token == c4_, 1.0, 0.0)[:, :TOK]
     nt = ((1,), (1,))
     wide = dot(widen.astype(BF16), table.astype(BF16), nt)
-    A[...] = jnp.where(q_r == q_c, wide, 0.0).astype(BF16)
+    wide = jnp.where(q_r == q_c, wide, 0.0)
+    A[...] = wide.astype(BF16)
+    AT[...] = wide.T.astype(BF16)
     gsb = jnp.broadcast_to(gsum, (128, TOK))
     grep[...] = dot(widen, gsb, nt, lax.Precision.HIGHEST)
     gslot[...] = dot(table, gsb, nt, lax.Precision.HIGHEST)
 
-    a1b(jnp.int32(0))
+    done(G.at[0, twin], gp_r.at[0])
+    a1b(jnp.int32(1))
 
     pre[...] = jnp.zeros_like(pre)
     gh[...] = jnp.zeros_like(gh)
@@ -148,7 +153,7 @@
         done(G.at[g, pl.ds(0, 288)], ge_r.at[g])
         scale = jnp.where(g < NC, 1.0, grep[...][:, :1])
         v = (G[g].astype(F32) * scale).astype(BF16)
-        packed = dot(A[...], v, ((0,), (0,))).astype(BF16)
+        packed = dot(AT[...], v).astype(BF16)
         own = block(z, yh)
         for q in range(4):
             R[g, own, q * QW : (q + 1) * QW] = packed[q * 32 : (q + 1) * 32]
@@ -215,7 +220,6 @@
 
     def a6(g):
         done(R.at[g, pl.ds(at16((1 - c) * HALF), HALF)], sib_r.at[g])
-        pltpu.make_async_copy(R.at[g], rg_hbm.at[g], hbm_s.at[g]).start()
 
         @pl.when(g == 0)
         def _():
@@ -224,16 +228,22 @@
 
         @pl.when(g < NC)
         def _():
-            pre[...] += dot(R[g], win[pl.ds(at16(g * CW, CW), CW), :])
+            where = pl.ds(at16(g * CW, CW), CW)
+            pre[...] += dot(R[g], win[where, :])
+            RT[where, :] = R[g].T
+            pltpu.make_async_copy(RT.at[where], rt_hbm.at[where], hbm_s.at[g]).start()
 
         @pl.when(g >= NC)
         def _():
+            pltpu.make_async_copy(R.at[g], sg_hbm.at[g - NC], hbm_s.at[g]).start()
             gh[...] += dot(R[g], wout[:, pl.ds(at16((g - NC) * CW, CW), CW)], ((1,), (1,)))
 
         @pl.when(g == NC - 1)
         def _():
             v = pre[...]
-            hid[...] = (v * jax.nn.sigmoid(v)).astype(BF16)
+            v = v * jax.nn.sigmoid(v)
+            hid[...] = v.astype(BF16)
+            hidt[...] = v.T.astype(BF16)
 
         @pl.when(g == 2 * NC - 1)
         def _():
@@ -423,7 +433,7 @@
     def step(t, carry):
         stage(a1, t + LEAD)
         stage(a2, t)
-        stage(a1b, t + 1)
+        stage(a1b, t + 2)
         stage(a3, t - LAG3)
         stage(a4, t - LAG4)
         stage(a5, t - LAG5)
@@ -444,7 +454,7 @@
     def finish(g, carry):
         done(G.at[g, pl.ds(0, 336)], ge_s.at[g])
         done(R.at[g, pl.ds(0, 480)], ag_s.at[g])
-        pltpu.make_async_copy(R.at[g], rg_hbm.at[g], hbm_s.at[g]).wait()
+        done(R.at[g], hbm_s.at[g])
         return carry
 
     lax.fori_loop(0, 2 * NC, finish, 0)
@@ -461,35 +471,39 @@
         done(FB.at[slot], fb_s.at[slot])
 
 
-def grads(rows, slot_grad, hid, gp, gin, gout):
-    gin[...] = dot(rows[0], gp[...], ((0,), (0,))).astype(BF16)
-    gout[...] = dot(hid[...], slot_grad[0], ((0,), (0,))).astype(BF16)
+def grads(rows_t, slot_grad, hid_t, gp, gin, gout):
+    gin[...] = dot(rows_t[...], gp[...]).astype(BF16)
+    gout[...] = dot(hid_t[...], slot_grad[0]).astype(BF16)
 
 
 def local(tokens, cotangent, expert_ids, gate_values, w_in, w_out):
     vmem, hbm = pl.BlockSpec(memory_space=pltpu.VMEM), pl.BlockSpec(memory_space=pl.ANY)
     dma = lambda n: pltpu.SemaphoreType.DMA((n,))
-    layer_out, grad_tokens, rg, hid, gp = pl.pallas_call(
+    layer_out, grad_tokens, rows_t, slot_grad, hid_t, gp = pl.pallas_call(
         exchange,
         name="exchange",
         out_shape=(
             jax.ShapeDtypeStruct((12, D), BF16),
             jax.ShapeDtypeStruct((12, D), BF16),
-            jax.ShapeDtypeStruct((2 * NC, ROWS, CW), BF16),
+            jax.ShapeDtypeStruct((D, ROWS), BF16),
+            jax.ShapeDtypeStruct((NC, ROWS, CW), BF16),
             jax.ShapeDtypeStruct((ROWS, HID), BF16),
             jax.ShapeDtypeStruct((ROWS, HID), BF16),
         ),
         in_specs=[vmem, vmem, vmem, vmem, hbm, hbm],
-        out_specs=(vmem, vmem, hbm, vmem, vmem),
+        out_specs=(vmem, vmem, hbm, hbm, vmem, vmem),
         scratch_shapes=[
             pltpu.VMEM((D, HID), BF16),
             pltpu.VMEM((HID, D), BF16),
             pltpu.VMEM((2 * NC, 48, QW), BF16),
             pltpu.VMEM((2 * NC, 4 * TOK, QW), BF16),
             pltpu.VMEM((2 * NC, ROWS, CW), BF16),
+            pltpu.VMEM((D, ROWS), BF16),
+            pltpu.VMEM((ROWS, HID), BF16),
             pltpu.VMEM((ROWS, HID), F32),
             pltpu.VMEM((ROWS, HID), F32),
             pltpu.VMEM((4 * TOK, 128), BF16),
+            pltpu.VMEM((128, 4 * TOK), BF16),
             pltpu.VMEM((4 * TOK, 128), F32),
             pltpu.VMEM((128, 128), F32),
             pltpu.VMEM((2, HALF, CW), BF16),
@@ -516,7 +530,6 @@
             collective_id=0, has_side_effects=True, vmem_limit_bytes=56 * 2**20
         ),
     )(tokens, cotangent, expert_ids.T, gate_values.T, w_in[0], w_out[0])
-    one = lambda f: pl.BlockSpec((1, ROWS, CW), f)
     grad_in, grad_out = pl.pallas_call(
         grads,
         name="grads",
@@ -526,8 +539,8 @@
             jax.ShapeDtypeStruct((HID, D), BF16),
         ),
         in_specs=[
-            one(lambda k: (k, 0, 0)),
-            one(lambda k: (NC + k, 0, 0)),
+            pl.BlockSpec((CW, ROWS), lambda k: (k, 0)),
+            pl.BlockSpec((1, ROWS, CW), lambda k: (k, 0, 0)),
             pl.BlockSpec((ROWS, HID), lambda k: (0, 0)),
             pl.BlockSpec((ROWS, HID), lambda k: (0, 0)),
         ],
@@ -536,7 +549,7 @@
             pl.BlockSpec((HID, CW), lambda k: (0, k)),
         ),
         compiler_params=pltpu.CompilerParams(vmem_limit_bytes=62 * 2**20),
-    )(rg, rg, hid, gp)
+    )(rows_t, slot_grad, hid_t, gp)
     return layer_out, grad_tokens, grad_in[None], grad_out[None]
 
 

time: 155 us -> 144 us (0.929)
  Pallas kernels: 152 us -> 142 us
    pallas_call x1, Pallas kernels: 139 us -> 129 us  [local(): pl.pallas_call(exchange, name='exchange', out_shape=(jax.ShapeDtypeStruct...]
where the time goes in v3:
time: 144 us
  Pallas kernels  142 us (99%)
    pallas_call x1, Pallas kernels, local(): pl.pallas_call(exchange, name='exchange', out_shape=(jax.ShapeDtypeStruct...  129 us
    pallas_call x1, Pallas kernels, local(): pl.pallas_call(grads, name='grads', grid=(NC,), out_shape=(jax.ShapeDtype...  13.1 us

profile of v3, /device:TPU:0, one launch (start us, length us, event | category | flops | bytes accessed | tf_op | source)
XLA Modules:
  0.0 143.7 jit_solution(12084080914324975716)
XLA Ops:
  0.6 128.6 %exchange.1 = (bf16[12,6144]{1,0:T(8,128)(2,1)}, bf16[12,6144]{1,0:T(8,128)(2,1)}, bf16[6144,512]{1,0:T(8,128)(2,1)}, bf16[6,512,1024]{2,1,0:T(8,128)(2,1)}, bf1...) custom-call(bf16[12,6144]{1,0:T(8,128)(2,1)} %tok_ref.1, bf16[12,6144]{1,0:T(8,128)(2,1)} %cot_ref.1, s32[2,96]{1,0:T(2,128)} %bitcast.8, ...), custom_call_target="tpu_custom_call" | custom-call | tf_op jit(solution)/shard_map/exchange/pallas_call | solution.py:482
  129.2 0.0 copy-start.1
  129.2 0.0 copy-start
  129.2 13.1 %grads.1 = (bf16[6144,512]{1,0:T(8,128)(2,1)}, bf16[512,6144]{1,0:T(8,128)(2,1)}) custom-call(bf16[6144,512]{1,0:T(8,128)(2,1)} %get-tuple-element.14.rows_t, bf16[6,512,1024]{2,1,0:T(8,128)(2,1)} %get-tuple-element.15.slot_grad, bf16[512,512]{1,0:T(8,128)(2,1)} %get-tuple-element.16.hid_t, bf16[512,512]{1,0:T(8,128)(2,1)} %get-tuple-element.17.gp), custom_call_target="tpu_custom_call" | custom-call | tf_op jit(solution)/shard_map/grads/pallas_call | solution.py:533
  142.3 0.0 copy-done.1
  142.3 0.7 copy.12
  143.0 0.0 copy-done
  143.0 0.7 copy.13
Async XLA Ops:
  129.2 13.1 %copy-start.1 = (bf16[12,6144]{1,0:T(8,128)(2,1)S(1)}, bf16[12,6144]{1,0:T(8,128)(2,1)}, u32[]{:S(2)}) copy-start(bf16[12,6144]{1,0:T(8,128)(2,1)} %get-tuple-element.24) | copy-start | bytes 442372
  129.2 13.8 %copy-start = (bf16[12,6144]{1,0:T(8,128)(2,1)S(1)}, bf16[12,6144]{1,0:T(8,128)(2,1)}, u32[]{:S(2)}) copy-start(bf16[12,6144]{1,0:T(8,128)(2,1)} %get-tuple-element.25) | copy-start | bytes 442372

commit v4 on v3

--- a/solution.py
+++ b/solution.py
@@ -16,11 +16,11 @@
 ROWS = 512
 HALF = 256
 DEP = 6
-MOD, WHICH = 3, 2
+MOD, WHICH = 3, 0
 LEAD = 3
 LAG3, LAG4, LAG5, LAGY, LAG6 = 1, 3, 5, 6, 7
 OFF = NC + LAG6
-L2, L3, L4, L5, L6, L7 = 1, 3, 5, 7, 9, 11
+L2, L3, L4, L5, L6, L7 = 1, 3, 5, 7, 10, 13
 STEPS = OFF + 2 * NC + L7
 MESH = pl.DeviceIdType.MESH
 F32, BF16 = jnp.float32, jnp.bfloat16
@@ -473,7 +473,8 @@
 
 def grads(rows_t, slot_grad, hid_t, gp, gin, gout):
     gin[...] = dot(rows_t[...], gp[...]).astype(BF16)
-    gout[...] = dot(hid_t[...], slot_grad[0]).astype(BF16)
+    for i in range(2):
+        gout[:, i * CW : (i + 1) * CW] = dot(hid_t[...], slot_grad[i]).astype(BF16)
 
 
 def local(tokens, cotangent, expert_ids, gate_values, w_in, w_out):
@@ -533,20 +534,20 @@
     grad_in, grad_out = pl.pallas_call(
         grads,
         name="grads",
-        grid=(NC,),
+        grid=(NC // 2,),
         out_shape=(
             jax.ShapeDtypeStruct((D, HID), BF16),
             jax.ShapeDtypeStruct((HID, D), BF16),
         ),
         in_specs=[
-            pl.BlockSpec((CW, ROWS), lambda k: (k, 0)),
-            pl.BlockSpec((1, ROWS, CW), lambda k: (k, 0, 0)),
+            pl.BlockSpec((2 * CW, ROWS), lambda k: (k, 0)),
+            pl.BlockSpec((2, ROWS, CW), lambda k: (k, 0, 0)),
             pl.BlockSpec((ROWS, HID), lambda k: (0, 0)),
             pl.BlockSpec((ROWS, HID), lambda k: (0, 0)),
         ],
         out_specs=(
-            pl.BlockSpec((CW, HID), lambda k: (k, 0)),
-            pl.BlockSpec((HID, CW), lambda k: (0, k)),
+            pl.BlockSpec((2 * CW, HID), lambda k: (k, 0)),
+            pl.BlockSpec((HID, 2 * CW), lambda k: (0, k)),
         ),
         compiler_params=pltpu.CompilerParams(vmem_limit_bytes=62 * 2**20),
     )(rows_t, slot_grad, hid_t, gp)

time: 144 us -> 141 us (0.979)
  Pallas kernels: 142 us -> 139 us
    pallas_call x1, Pallas kernels: 129 us -> 126 us  [local(): pl.pallas_call(exchange, name='exchange', out_shape=(jax.ShapeDtypeStruct...]
where the time goes in v4:
time: 141 us
  Pallas kernels  139 us (99%)
    pallas_call x1, Pallas kernels, local(): pl.pallas_call(exchange, name='exchange', out_shape=(jax.ShapeDtypeStruct...  126 us
    pallas_call x1, Pallas kernels, local(): pl.pallas_call(grads, name='grads', grid=(NC // 2,), out_shape=(jax.Shape...  12.9 us

profile of v4, /device:TPU:0, one launch (start us, length us, event | category | flops | bytes accessed | tf_op | source)
XLA Modules:
  0.0 141.0 jit_solution(14679806192740597600)
XLA Ops:
  0.6 126.0 %exchange.1 = (bf16[12,6144]{1,0:T(8,128)(2,1)}, bf16[12,6144]{1,0:T(8,128)(2,1)}, bf16[6144,512]{1,0:T(8,128)(2,1)}, bf16[6,512,1024]{2,1,0:T(8,128)(2,1)}, bf1...) custom-call(bf16[12,6144]{1,0:T(8,128)(2,1)} %tok_ref.1, bf16[12,6144]{1,0:T(8,128)(2,1)} %cot_ref.1, s32[2,96]{1,0:T(2,128)} %bitcast.8, ...), custom_call_target="tpu_custom_call" | custom-call | tf_op jit(solution)/shard_map/exchange/pallas_call | solution.py:483
  126.6 0.0 copy-start.1
  126.7 0.0 copy-start
  126.7 12.9 %grads.1 = (bf16[6144,512]{1,0:T(8,128)(2,1)}, bf16[512,6144]{1,0:T(8,128)(2,1)}) custom-call(bf16[6144,512]{1,0:T(8,128)(2,1)} %get-tuple-element.14.rows_t, bf16[6,512,1024]{2,1,0:T(8,128)(2,1)} %get-tuple-element.15.slot_grad, bf16[512,512]{1,0:T(8,128)(2,1)} %get-tuple-element.16.hid_t, bf16[512,512]{1,0:T(8,128)(2,1)} %get-tuple-element.17.gp), custom_call_target="tpu_custom_call" | custom-call | tf_op jit(solution)/shard_map/grads/pallas_call | solution.py:534
  139.6 0.0 copy-done.1
  139.6 0.7 copy.12
  140.3 0.0 copy-done
  140.3 0.7 copy.13
Async XLA Ops:
  126.6 13.0 %copy-start.1 = (bf16[12,6144]{1,0:T(8,128)(2,1)S(1)}, bf16[12,6144]{1,0:T(8,128)(2,1)}, u32[]{:S(2)}) copy-start(bf16[12,6144]{1,0:T(8,128)(2,1)} %get-tuple-element.24) | copy-start | bytes 442372
  126.7 13.6 %copy-start = (bf16[12,6144]{1,0:T(8,128)(2,1)S(1)}, bf16[12,6144]{1,0:T(8,128)(2,1)}, u32[]{:S(2)}) copy-start(bf16[12,6144]{1,0:T(8,128)(2,1)} %get-tuple-element.25) | copy-start | bytes 442372
